TPU v7x, 512 devices: a whole 4x8x8 slice. The times are simulated.
512 devices in a mesh: queue: 64 (over z, y_lo, x), space: 8 (over y_hi, core).
Axes of the slice: x: 4, y: 8 (y_hi: 4, y_lo: 2; y = y_hi * 2 + y_lo), z: 8, core: 2. Of those that a mesh axis runs over, the one named last changes fastest.
Arguments:
- queries: bfloat16 [64, 1024, 1536], P('queue', 'space'), as said below
- keys: bfloat16 [64, 1024, 1536], P('queue', 'space'), as said below
- values: bfloat16 [64, 1024, 1536], P('queue', 'space'), may hold values from -6 to 6
- levels: int32 [64], P('queue'), may hold values from 0 to 63
- plan: int32 [64], replicated, may hold values from 0 to 127
- gate_table: float32 [128, 1536], replicated, may hold values from -5 to 5
- fresh: bfloat16 [1024, 1536], P('space'), may hold values from -6 to 6
Outputs:
- denoised: bfloat16 [64, 1024, 1536], P('queue', 'space')
- queue_next: bfloat16 [64, 1024, 1536], P('queue', 'space')
Inputs may be any that keep to these rules, and one draw needn't show every extreme that they name: Most keys are of order one; a few key rows may nearly equal a neighbouring key row of the same frame. Most queries are of order one; a few query rows may be up to 40 times a key row of the same frame, so that single scores can reach a few hundred.
All inputs are finite; a program needn't handle non-finite values.
Results may differ from a plain program's by a relative error of at most 0.0057.
Values may be sent and summed in bfloat16 or wider, within the bound.
A program may use at most 64 MiB of HBM per device.

v0:
```python
import jax
import jax.numpy as jnp
from jax import lax
from jax.sharding import PartitionSpec as P

HEADS = 24
HEAD_SIZE = 64


def passed_along(array, axis, by):
    size = lax.axis_size(axis)
    pairs = [(i, i + by) for i in range(size) if 0 <= i + by < size]
    return lax.ppermute(array, axis, pairs)


def body(queries, keys, values, levels, plan, gate_table, fresh):
    parts = lax.axis_size("space")
    local_heads = HEADS // parts
    width = local_heads * HEAD_SIZE
    rows = queries.shape[1]
    frame_len = rows * parts

    def split_heads(array):
        return array[0].reshape(rows, parts, width)

    def as_heads(array):
        return array.reshape(frame_len, local_heads, HEAD_SIZE)

    moved = (
        lax.all_to_all(split_heads(queries), "space", split_axis=1, concat_axis=0, tiled=True),
        lax.all_to_all(split_heads(keys), "space", split_axis=1, concat_axis=0, tiled=True),
        lax.all_to_all(split_heads(values), "space", split_axis=1, concat_axis=0, tiled=True),
    )
    query_all, key_own, value_own = [as_heads(item) for item in moved]
    key_prev, value_prev = passed_along((key_own, value_own), "queue", 1)
    key_all = jnp.concatenate([key_own, key_prev], 0)
    value_all = jnp.concatenate([value_own, value_prev], 0)
    first_frame = lax.axis_index("queue") == 0
    masked = first_frame & (jnp.arange(2 * frame_len) >= frame_len)
    block = min(512, frame_len)

    def attend(query_block):
        scores = jnp.einsum(
            "qhd,khd->hqk", query_block, key_all, preferred_element_type=jnp.float32
        ) * HEAD_SIZE ** (-0.5)
        scores = jnp.where(masked[None, None, :], -jnp.inf, scores)
        top = jnp.max(scores, axis=-1, keepdims=True)
        expo = jnp.exp(scores - top)
        total = jnp.sum(expo, axis=-1)
        probs = expo.astype(jnp.bfloat16)
        mixed = jnp.einsum("hqk,khd->qhd", probs, value_all, preferred_element_type=jnp.float32)
        return (mixed / jnp.swapaxes(total, 0, 1)[:, :, None]).astype(jnp.bfloat16)

    blocks = query_all.reshape(frame_len // block, block, local_heads, HEAD_SIZE)
    attended = lax.map(attend, blocks).reshape(frame_len, 1, width)
    restored = lax.all_to_all(attended, "space", split_axis=0, concat_axis=1, tiled=True).reshape(
        rows, parts * width
    )
    level_hit = jnp.arange(plan.shape[0]) == levels[0]
    step_now = jnp.sum(jnp.where(level_hit, plan, 0))
    step_hit = (jnp.arange(gate_table.shape[0]) == step_now).astype(jnp.float32)
    gate = jnp.dot(step_hit, gate_table, precision=lax.Precision.HIGHEST)
    denoised = (gate[None, :] * restored.astype(jnp.float32)).astype(jnp.bfloat16)
    ahead = passed_along(denoised, "queue", -1)
    last_slot = lax.axis_index("queue") == lax.axis_size("queue") - 1
    queue_next = jnp.where(last_slot, fresh, ahead)
    return (denoised[None], queue_next[None])


def solution(mesh):
    return jax.shard_map(
        body,
        mesh=mesh,
        in_specs=(
            P("queue", "space", None),
            P("queue", "space", None),
            P("queue", "space", None),
            P("queue"),
            P(),
            P(),
            P("space", None),
        ),
        out_specs=(P("queue", "space", None), P("queue", "space", None)),
        check_vma=False,
    )
```

profile of v0, /device:TPU:136, one launch (start us, length us, event | category | flops | bytes accessed | tf_op | source)
XLA Modules:
  0.0 135.4 jit_solution(7341803461664635962)
XLA Ops:
  0.6 2.0 %copy.52 = bf16[1,128,1536]{1,2,0:T(8,128)(2,1)} copy(bf16[1,128,1536]{2,1,0:T(8,128)(2,1)} %param.10) | data formatting | bytes 786432 | tf_op args[1]
  2.6 6.2 %all-to-all-start.1 = ((bf16[128,8,192]{0,2,1:T(8,128)(2,1)}), bf16[128,8,192]{0,2,1:T(8,128)(2,1)S(1)}, u32[]{:S(2)}, u32[]{:S(2)}) async-start(bf16[128,8,192]{0,2,1:T(8,128)(2,1)} %bitcast.5), calls=%async_computation.1 | async-start | bytes 786432 | tf_op jit(solution)/shard_map/all_to_all | solution.py:31
  8.8 1.9 %copy.54 = bf16[1,128,1536]{1,2,0:T(8,128)(2,1)} copy(bf16[1,128,1536]{2,1,0:T(8,128)(2,1)} %param.11) | data formatting | bytes 786432 | tf_op args[2]
  10.8 13.5 %all-to-all-done.1 = bf16[128,8,192]{0,2,1:T(8,128)(2,1)S(1)} async-done(((bf16[128,8,192]{0,2,1:T(8,128)(2,1)}), bf16[128,8,192]{0,2,1:T(8,128)(2,1)S(1)}, u32[]{:S(2)}, u32[]{:S(2)}) %all-to-all-start.1) | async-done | bytes 393248 | tf_op jit(solution)/shard_map/all_to_all | solution.py:31
  24.3 3.5 %all-to-all-start.2 = ((bf16[128,8,192]{0,2,1:T(8,128)(2,1)}), bf16[128,8,192]{0,2,1:T(8,128)(2,1)S(1)}, u32[]{:S(2)}, u32[]{:S(2)}) async-start(bf16[128,8,192]{0,2,1:T(8,128)(2,1)} %bitcast.8), calls=%async_computation.2 | async-start | bytes 786432 | tf_op jit(solution)/shard_map/all_to_all | solution.py:32
  27.8 1.9 %copy.50 = bf16[1,128,1536]{1,2,0:T(8,128)(2,1)} copy(bf16[1,128,1536]{2,1,0:T(8,128)(2,1)} %param.9) | data formatting | bytes 786432 | tf_op args[0]
  29.7 13.0 %all-to-all-done.2 = bf16[128,8,192]{0,2,1:T(8,128)(2,1)S(1)} async-done(((bf16[128,8,192]{0,2,1:T(8,128)(2,1)}), bf16[128,8,192]{0,2,1:T(8,128)(2,1)S(1)}, u32[]{:S(2)}, u32[]{:S(2)}) %all-to-all-start.2) | async-done | bytes 393248 | tf_op jit(solution)/shard_map/all_to_all | solution.py:32
  42.7 3.5 %all-to-all-start = ((bf16[128,8,192]{0,2,1:T(8,128)(2,1)}), bf16[128,8,192]{0,2,1:T(8,128)(2,1)S(1)}, u32[]{:S(2)}, u32[]{:S(2)}) async-start(bf16[128,8,192]{0,2,1:T(8,128)(2,1)} %bitcast.2), calls=%async_computation | async-start | bytes 786432 | tf_op jit(solution)/shard_map/all_to_all | solution.py:30
  46.6 3.4 %collective-permute-start = (bf16[1024,3,64]{0,2,1:T(8,128)(2,1)S(1)}, bf16[1024,3,64]{0,2,1:T(8,128)(2,1)S(1)}, u32[]{:S(2)}, u32[]{:S(2)}) collective-permute-start(bf16[1024,3,64]{0,2,1:T(8,128)(2,1)S(1)} %reshape.67), channel_id=1, source_target_pairs={{0,8},{8,16},{16,24},{24,32},{32,40},{40,48},{48,56},{56,64},{64,7... | collective-permute-start | bytes 1179656 | tf_op jit(solution)/shard_map/ppermute | solution.py:13
  50.5 3.4 %collective-permute-start.1 = (bf16[1024,3,64]{0,2,1:T(8,128)(2,1)S(1)}, bf16[1024,3,64]{0,2,1:T(8,128)(2,1)}, u32[]{:S(2)}, u32[]{:S(2)}) collective-permute-start(bf16[1024,3,64]{0,2,1:T(8,128)(2,1)S(1)} %reshape.68), channel_id=1, source_target_pairs={{0,8},{8,16},{16,24},{24,32},{32,40},{40,48},{48,56},{56,64},{64,7... | collective-permute-start | bytes 1179656 | tf_op jit(solution)/shard_map/ppermute | solution.py:13
  53.9 7.6 %all-to-all-done = bf16[128,8,192]{0,2,1:T(8,128)(2,1)S(1)} async-done(((bf16[128,8,192]{0,2,1:T(8,128)(2,1)}), bf16[128,8,192]{0,2,1:T(8,128)(2,1)S(1)}, u32[]{:S(2)}, u32[]{:S(2)}) %all-to-all-start) | async-done | bytes 393248 | tf_op jit(solution)/shard_map/all_to_all | solution.py:30
  61.9 6.3 %collective-permute-done = bf16[1024,3,64]{0,2,1:T(8,128)(2,1)S(1)} collective-permute-done((bf16[1024,3,64]{0,2,1:T(8,128)(2,1)S(1)}, bf16[1024,3,64]{0,2,1:T(8,128)(2,1)S(1)}, u32[]{:S(2)}, u32[]{:S(2)}) %collective-permute-start) | collective-permute-done | bytes 393248 | tf_op jit(solution)/shard_map/ppermute | solution.py:13
  68.3 8.2 %collective-permute-done.1 = bf16[1024,3,64]{0,2,1:T(8,128)(2,1)} collective-permute-done((bf16[1024,3,64]{0,2,1:T(8,128)(2,1)S(1)}, bf16[1024,3,64]{0,2,1:T(8,128)(2,1)}, u32[]{:S(2)}, u32[]{:S(2)}) %collective-permute-start.1) | collective-permute-done | bytes 393248 | tf_op jit(solution)/shard_map/ppermute | solution.py:13
  76.5 1.0 pad_maximum_fusion.1
  77.6 17.1 %while.11 = (s32[]{:T(128)}, bf16[2,512,3,64]{1,3,2,0:T(8,128)(2,1)}, bf16[2,512,3,64]{1,3,2,0:T(8,128)(2,1)S(1)}, bf16[2048,3,64]{0,2,1:T(8,128)(2,1)S(1)}, bf1...) while((s32[]{:T(128)}, bf16[2,512,3,64]{1,3,2,0:T(8,128)(2,1)}, ...), condition=%wide.region_4.5_spmd.clone, body=%wide.region_1.4_spmd.clone.sunk | while | flops 840107008 | bytes 42903692 | solution.py:55
  77.6 2.0 %fusion.51 = (f32[3,512]{1,0:T(4,128)S(1)}, f32[3,512,2048]{2,1,0:T(8,128)S(1)}) fusion(pred[2048]{0:T(1024)(128)(4,1)S(1)} %fusion.50, bf16[2048,3,64]{0,2,1:T(8,128)(2,1)S(1)} %get-tuple-element.154, bf16[2,512,3,64]{1,3,2,0:T(8,128)(2,1)S(1)} %get-tuple-element.153, s32[]{:T(128)} %get-tuple-element.144), kind=kOutput, calls=%fused_computation.3.clone.1 | convolution fusion | flops 412088832 | bytes 13574148 | tf_op jit(solution)/shard_map/while/body/eval_jaxpr/qhd,khd->hqk/dot_general | solution.py:43
  79.6 2.8 %fusion.52 = f32[3,512]{1,0:T(4,128)S(1)} fusion(f32[3,512,2048]{2,1,0:T(8,128)S(1)} %get-tuple-element.135, f32[3,512]{1,0:T(4,128)S(1)} %get-tuple-element.136, pred[2048]{0:T(1024)(128)(4,1)S(1)} %fusion.50), kind=kLoop, calls=%fused_computation.4.clone.1 | loop fusion | flops 12581376 | bytes 12597248 | tf_op jit(solution)/shard_map/while/body/eval_jaxpr/reduce_sum | solution.py:49
  82.4 3.0 %fusion.53 = bf16[2,512,3,64]{1,3,2,0:T(8,128)(2,1)S(1)} fusion(bf16[2,512,3,64]{1,3,2,0:T(8,128)(2,1)S(1)} %copy-done.2, s32[]{:T(128)} %get-tuple-element.144, bf16[2048,3,64]{0,2,1:T(8,128)(2,1)S(1)} %get-tuple-element.155, f32[3,512,2048]{2,1,0:T(8,128)S(1)} %get-tuple-element.135, f32[3,512]{1,0:T(4,128)S(1)} %get-tuple-element.136, ...), kind=kOutput, calls=%fused_computation.12.clone.1 | convolution fusion | flops 415432704 | bytes 13584388 | tf_op jit(solution)/shard_map/while/body/eval_jaxpr/hqk,khd->qhd/dot_general | solution.py:51
  86.2 2.0 %fusion.51 = (f32[3,512]{1,0:T(4,128)S(1)}, f32[3,512,2048]{2,1,0:T(8,128)S(1)}) fusion(pred[2048]{0:T(1024)(128)(4,1)S(1)} %fusion.50, bf16[2048,3,64]{0,2,1:T(8,128)(2,1)S(1)} %get-tuple-element.154, bf16[2,512,3,64]{1,3,2,0:T(8,128)(2,1)S(1)} %get-tuple-element.153, s32[]{:T(128)} %get-tuple-element.144), kind=kOutput, calls=%fused_computation.3.clone.1 | convolution fusion | flops 412088832 | bytes 13574148 | tf_op jit(solution)/shard_map/while/body/eval_jaxpr/qhd,khd->hqk/dot_general | solution.py:43
  88.1 2.8 %fusion.52 = f32[3,512]{1,0:T(4,128)S(1)} fusion(f32[3,512,2048]{2,1,0:T(8,128)S(1)} %get-tuple-element.135, f32[3,512]{1,0:T(4,128)S(1)} %get-tuple-element.136, pred[2048]{0:T(1024)(128)(4,1)S(1)} %fusion.50), kind=kLoop, calls=%fused_computation.4.clone.1 | loop fusion | flops 12581376 | bytes 12597248 | tf_op jit(solution)/shard_map/while/body/eval_jaxpr/reduce_sum | solution.py:49
  90.9 3.0 %fusion.53 = bf16[2,512,3,64]{1,3,2,0:T(8,128)(2,1)S(1)} fusion(bf16[2,512,3,64]{1,3,2,0:T(8,128)(2,1)S(1)} %copy-done.2, s32[]{:T(128)} %get-tuple-element.144, bf16[2048,3,64]{0,2,1:T(8,128)(2,1)S(1)} %get-tuple-element.155, f32[3,512,2048]{2,1,0:T(8,128)S(1)} %get-tuple-element.135, f32[3,512]{1,0:T(4,128)S(1)} %get-tuple-element.136, ...), kind=kOutput, calls=%fused_computation.12.clone.1 | convolution fusion | flops 415432704 | bytes 13584388 | tf_op jit(solution)/shard_map/while/body/eval_jaxpr/hqk,khd->qhd/dot_general | solution.py:51
  94.7 1.4 %copy.57 = bf16[2,512,3,64]{1,0,3,2:T(2,128)(2,1)S(1)} copy(bf16[2,512,3,64]{1,3,2,0:T(8,128)(2,1)} %get-tuple-element.34) | data formatting | bytes 786432 | tf_op jit(solution)/shard_map/while | solution.py:55
  96.9 0.9 reduce.2
  98.0 1.3 reshape.77
  99.3 6.3 %all-to-all-start.3 = ((bf16[8,2,12288]{2,1,0:T(2,128)(2,1)}), bf16[8,2,12288]{2,1,0:T(2,128)(2,1)S(1)}, u32[]{:S(2)}, u32[]{:S(2)}) async-start(bf16[8,2,12288]{2,1,0:T(2,128)(2,1)} %reshape.77), calls=%async_computation.3 | async-start | bytes 786432 | tf_op jit(solution)/shard_map/all_to_all | solution.py:56
  107.2 1.0 convolution_reduce_fusion
  108.2 11.5 %all-to-all-done.3 = bf16[8,2,12288]{2,1,0:T(2,128)(2,1)S(1)} async-done(((bf16[8,2,12288]{2,1,0:T(2,128)(2,1)}), bf16[8,2,12288]{2,1,0:T(2,128)(2,1)S(1)}, u32[]{:S(2)}, u32[]{:S(2)}) %all-to-all-start.3) | async-done | bytes 393248 | tf_op jit(solution)/shard_map/all_to_all | solution.py:56
  119.7 0.7 reshape.78
  121.7 2.6 %collective-permute-start.2 = (bf16[128,1536]{0,1:T(8,128)(2,1)S(1)}, bf16[128,1536]{0,1:T(8,128)(2,1)S(1)}, u32[]{:S(2)}, u32[]{:S(2)}) collective-permute-start(bf16[128,1536]{0,1:T(8,128)(2,1)S(1)} %fusion.30), channel_id=1, source_target_pairs={{8,0},{16,8},{24,16},{32,24},{40,32},{48,40},{56,48},{64,56},{72,6... | collective-permute-start | bytes 1179656 | tf_op jit(solution)/shard_map/ppermute | solution.py:13
  124.6 0.9 copy.63
  125.6 8.8 %collective-permute-done.2 = bf16[128,1536]{0,1:T(8,128)(2,1)S(1)} collective-permute-done((bf16[128,1536]{0,1:T(8,128)(2,1)S(1)}, bf16[128,1536]{0,1:T(8,128)(2,1)S(1)}, u32[]{:S(2)}, u32[]{:S(2)}) %collective-permute-start.2) | collective-permute-done | bytes 393248 | tf_op jit(solution)/shard_map/ppermute | solution.py:13
  134.5 0.9 copy.64
  (37 shorter events, 6.3 us)
Async XLA Ops:
  0.6 106.6 %copy-start = (f32[128,1536]{1,0:T(8,128)S(1)}, f32[128,1536]{1,0:T(8,128)}, u32[]{:S(2)}) copy-start(f32[128,1536]{1,0:T(8,128)} %param.14) | copy-start | bytes 2359300
  2.6 21.7 %all-to-all-start.1 = ((bf16[128,8,192]{0,2,1:T(8,128)(2,1)}), bf16[128,8,192]{0,2,1:T(8,128)(2,1)S(1)}, u32[]{:S(2)}, u32[]{:S(2)}) async-start(bf16[128,8,192]{0,2,1:T(8,128)(2,1)} %bitcast.5), calls=%async_computation.1 | async-start | bytes 786432 | tf_op jit(solution)/shard_map/all_to_all | solution.py:31
  24.3 18.4 %all-to-all-start.2 = ((bf16[128,8,192]{0,2,1:T(8,128)(2,1)}), bf16[128,8,192]{0,2,1:T(8,128)(2,1)S(1)}, u32[]{:S(2)}, u32[]{:S(2)}) async-start(bf16[128,8,192]{0,2,1:T(8,128)(2,1)} %bitcast.8), calls=%async_computation.2 | async-start | bytes 786432 | tf_op jit(solution)/shard_map/all_to_all | solution.py:32
  42.7 18.7 %all-to-all-start = ((bf16[128,8,192]{0,2,1:T(8,128)(2,1)}), bf16[128,8,192]{0,2,1:T(8,128)(2,1)S(1)}, u32[]{:S(2)}, u32[]{:S(2)}) async-start(bf16[128,8,192]{0,2,1:T(8,128)(2,1)} %bitcast.2), calls=%async_computation | async-start | bytes 786432 | tf_op jit(solution)/shard_map/all_to_all | solution.py:30
  46.6 21.6 %collective-permute-start = (bf16[1024,3,64]{0,2,1:T(8,128)(2,1)S(1)}, bf16[1024,3,64]{0,2,1:T(8,128)(2,1)S(1)}, u32[]{:S(2)}, u32[]{:S(2)}) collective-permute-start(bf16[1024,3,64]{0,2,1:T(8,128)(2,1)S(1)} %reshape.67), channel_id=1, source_target_pairs={{0,8},{8,16},{16,24},{24,32},{32,40},{40,48},{48,56},{56,64},{64,7... | collective-permute-start | bytes 1179656 | tf_op jit(solution)/shard_map/ppermute | solution.py:13
  50.5 26.0 %collective-permute-start.1 = (bf16[1024,3,64]{0,2,1:T(8,128)(2,1)S(1)}, bf16[1024,3,64]{0,2,1:T(8,128)(2,1)}, u32[]{:S(2)}, u32[]{:S(2)}) collective-permute-start(bf16[1024,3,64]{0,2,1:T(8,128)(2,1)S(1)} %reshape.68), channel_id=1, source_target_pairs={{0,8},{8,16},{16,24},{24,32},{32,40},{40,48},{48,56},{56,64},{64,7... | collective-permute-start | bytes 1179656 | tf_op jit(solution)/shard_map/ppermute | solution.py:13
  77.6 28.7 %copy-start.1 = (bf16[128,1536]{1,0:T(8,128)(2,1)S(1)}, bf16[128,1536]{1,0:T(8,128)(2,1)}, u32[]{:S(2)}) copy-start(bf16[128,1536]{1,0:T(8,128)(2,1)} %param.15) | copy-start | bytes 1179652
  77.6 29.0 %copy-start.4 = (s32[64]{0:T(128)S(1)}, s32[64]{0:T(128)}, u32[]{:S(2)}) copy-start(s32[64]{0:T(128)} %param.13) | copy-start | bytes 772
  77.6 4.8 %copy-start.2 = (bf16[2,512,3,64]{1,3,2,0:T(8,128)(2,1)S(1)}, bf16[2,512,3,64]{1,3,2,0:T(8,128)(2,1)}, u32[]{:S(2)}) copy-start(bf16[2,512,3,64]{1,3,2,0:T(8,128)(2,1)} %get-tuple-element.145) | copy-start | bytes 1179652 | tf_op jit(solution)/shard_map/while
  85.4 0.7 copy-start.3
  86.1 4.8 %copy-start.2 = (bf16[2,512,3,64]{1,3,2,0:T(8,128)(2,1)S(1)}, bf16[2,512,3,64]{1,3,2,0:T(8,128)(2,1)}, u32[]{:S(2)}) copy-start(bf16[2,512,3,64]{1,3,2,0:T(8,128)(2,1)} %get-tuple-element.145) | copy-start | bytes 1179652 | tf_op jit(solution)/shard_map/while
  93.9 0.7 copy-start.3
  99.3 20.4 %all-to-all-start.3 = ((bf16[8,2,12288]{2,1,0:T(2,128)(2,1)}), bf16[8,2,12288]{2,1,0:T(2,128)(2,1)S(1)}, u32[]{:S(2)}, u32[]{:S(2)}) async-start(bf16[8,2,12288]{2,1,0:T(2,128)(2,1)} %reshape.77), calls=%async_computation.3 | async-start | bytes 786432 | tf_op jit(solution)/shard_map/all_to_all | solution.py:56
  121.7 12.7 %collective-permute-start.2 = (bf16[128,1536]{0,1:T(8,128)(2,1)S(1)}, bf16[128,1536]{0,1:T(8,128)(2,1)S(1)}, u32[]{:S(2)}, u32[]{:S(2)}) collective-permute-start(bf16[128,1536]{0,1:T(8,128)(2,1)S(1)} %fusion.30), channel_id=1, source_target_pairs={{8,0},{16,8},{24,16},{32,24},{40,32},{48,40},{56,48},{64,56},{72,6... | collective-permute-start | bytes 1179656 | tf_op jit(solution)/shard_map/ppermute | solution.py:13
where the time goes:
time: 136 us; the launch traced here: 135 us
  waiting for transfers between devices  69 us (51%)
  starting transfers between devices  28.9 us (21%)
  local copies, waits for them, and re-layouts  16.1 us (12%)
  matrix products  10.9 us (8%)
  other arithmetic  8.95 us (7%)
  between operations  1.53 us (1%)
    ppermute x3, waiting for transfers between devices, passed_along(): return lax.ppermute(array, axis, pairs)  23.4 us
    all_to_all x1, waiting for transfers between devices, body(): lax.all_to_all(split_heads(keys), 'space', split_axis=1, concat_axis=0, t...  13.5 us
    all_to_all x1, waiting for transfers between devices, body(): lax.all_to_all(split_heads(values), 'space', split_axis=1, concat_axis=0,...  13 us
    all_to_all x1, waiting for transfers between devices, body(): lax.all_to_all(attended, 'space', split_axis=0, concat_axis=1, tiled=True)  11.5 us
    unnamed x17, local copies, waits for them, and re-layouts  10.4 us
    ppermute x3, starting transfers between devices, passed_along(): return lax.ppermute(array, axis, pairs)  9.45 us
    all_to_all x1, waiting for transfers between devices, body(): lax.all_to_all(split_heads(queries), 'space', split_axis=1, concat_axis=0...  7.56 us
    all_to_all x1, starting transfers between devices, body(): lax.all_to_all(attended, 'space', split_axis=0, concat_axis=1, tiled=True)  6.31 us
  transfers between devices with their start and end apart: 7, of which 7 were waited for; matrix products, arithmetic and copies ran while one was open for 6% of the time, Pallas kernels for 0%

commit v1 on v0

v1 whole, which is shorter than its diff:
```python
import functools

import jax
import jax.numpy as jnp
from jax import lax
from jax.experimental import pallas as pl
from jax.experimental.pallas import tpu as pltpu
from jax.sharding import PartitionSpec as P

MESH = pl.DeviceIdType.MESH
BF16 = jnp.bfloat16
F32 = jnp.float32
ROWS = 128
HALF = 64
COLS = 1536
GROUPS = 8
FAR_FIRST = (4, 3, 5, 2, 6, 1, 7, 0)
PAIR_ORDER = (2, 1, 3, 0)
K, V, Q = 0, 1, 2


def dot_nt(a, b):
    return lax.dot_general(a, b, (((1,), (1,)), ((), ())), preferred_element_type=F32)


def left_lanes(shape):
    return lax.broadcasted_iota(jnp.int32, shape, len(shape) - 1) < HALF


def swap_halves(a):
    return pltpu.roll(a.astype(F32), HALF, a.ndim - 1).astype(a.dtype)


def tile_of(group):
    return 3 * (group // 2) + 2 * (group % 2)


def columns(tile):
    return pl.ds(pl.multiple_of(tile * 128, 128), 128)


def kernel(
    q_hbm, k_hbm, v_hbm, levels_ref, plan_ref, gate_hbm, fresh_hbm,
    den_ref, next_ref,
    src, packed, gate_buf,
    kt, vt, qt, kh, vh, qh,
    va, vb, ha, hb,
    ot, oh, ort, orh,
    in_sem, gate_sem,
    send_t, recv_t, send_h, recv_h,
    fwd_send_t, fwd_recv_t, fwd_send_h, fwd_recv_h,
    o_send_t, o_recv_t, o_send_h, o_recv_h,
    shift_send, shift_recv, fresh_sem,
):
    queue = lax.axis_index("queue")
    space = lax.axis_index("space")
    z, y_lo, x = queue // 8, (queue // 4) % 2, queue % 4
    y_hi, core = space // 2, space % 2
    y = y_hi * 2 + y_lo
    frame = z * 8 + core * 4 + x
    tokens_in = (kt, vt, qt)
    heads_in = (kh, vh, qh)

    def worker(of_frame, group):
        return (
            (of_frame // 8) * 8 + (group % 2) * 4 + of_frame % 4,
            (group // 2) * 2 + (of_frame // 4) % 2,
        )

    loads = [
        pltpu.make_async_copy(ref.at[0], src.at[i], in_sem.at[i])
        for i, ref in enumerate((k_hbm, v_hbm, q_hbm))
    ]
    for load in loads:
        load.start()
    gate_load = pltpu.make_async_copy(gate_hbm, gate_buf, gate_sem)
    gate_load.start()

    barrier = pltpu.get_barrier_semaphore()

    def greet(device):
        pl.semaphore_signal(barrier, inc=1, device_id=device, device_id_type=MESH)

    has_prev, has_next = frame > 0, frame < 63
    has_ahead, has_behind = queue > 0, queue < 63
    owns = core == y_lo
    for i in range(8):
        @pl.when(jnp.logical_not(owns & (space == i)))
        def _():
            greet((frame, i))
    pl.when(has_prev)(lambda: greet(worker(frame - 1, y)))
    pl.when(has_behind)(lambda: greet((queue + 1, space)))
    for i in range(GROUPS):
        @pl.when(jnp.logical_not(owns & (y == i)))
        def _():
            greet(worker(queue, i))
    greeted = (
        16
        - 2 * owns.astype(jnp.int32)
        + has_next.astype(jnp.int32)
        + has_ahead.astype(jnp.int32)
    )

    def pack(i):
        left = left_lanes((HALF, 128))
        for pair in range(4):
            tile = src[i, :, (3 * pair + 1) * 128 : (3 * pair + 2) * 128]
            top, bottom = tile[:HALF], tile[HALF:]
            packed[i, 2 * pair] = jnp.where(left, top, swap_halves(bottom))
            packed[i, 2 * pair + 1] = jnp.where(left, swap_halves(top), bottom)

    for i in (K, V, Q):
        loads[i].wait()
        pack(i)
    pl.semaphore_wait(barrier, greeted)

    def rows_of(index, size):
        return pl.ds(pl.multiple_of(index * size, size), size)

    def sent_tile(i, group):
        return pltpu.make_async_remote_copy(
            src_ref=src.at[i, :, columns(tile_of(group))],
            dst_ref=tokens_in[i].at[rows_of(space, ROWS)],
            send_sem=send_t.at[i, group], recv_sem=recv_t.at[i, space],
            device_id=worker(queue, group), device_id_type=MESH,
        )

    def sent_head(i, group):
        return pltpu.make_async_remote_copy(
            src_ref=packed.at[i, group],
            dst_ref=heads_in[i].at[rows_of(space, HALF)],
            send_sem=send_h.at[i, group], recv_sem=recv_h.at[i, space],
            device_id=worker(queue, group), device_id_type=MESH,
        )

    def send_out(make, kept, i):
        for shift in FAR_FIRST:
            group = (y + shift) % GROUPS
            if shift:
                make(i, group).start()
            else:
                pl.when(owns)(lambda: kept(i).start())
                pl.when(jnp.logical_not(owns))(lambda: make(i, group).start())

    def kept_tile(i):
        return pltpu.make_async_copy(
            src.at[i, :, columns(tile_of(y))],
            tokens_in[i].at[rows_of(space, ROWS)],
            recv_t.at[i, space],
        )

    def kept_head(i):
        return pltpu.make_async_copy(
            packed.at[i, y],
            heads_in[i].at[rows_of(space, HALF)],
            recv_h.at[i, space],
        )

    with jax.named_scope("send_all"):
        for i in (K, V, Q):
            send_out(sent_tile, kept_tile, i)
        for i in (K, V, Q):
            send_out(sent_head, kept_head, i)

    def arrival_tile(i, shard):
        return pltpu.make_async_copy(
            tokens_in[i].at[rows_of(shard, ROWS)], tokens_in[i].at[rows_of(shard, ROWS)], recv_t.at[i, shard]
        )

    def arrival_head(i, shard):
        return pltpu.make_async_copy(
            heads_in[i].at[rows_of(shard, HALF)], heads_in[i].at[rows_of(shard, HALF)], recv_h.at[i, shard]
        )

    def forward(buf, i, pair, size, sends, recvs):
        return pltpu.make_async_remote_copy(
            src_ref=buf.at[rows_of(pair, 2 * size)],
            dst_ref=buf.at[rows_of(4 + pair, 2 * size)],
            send_sem=sends.at[i, pair], recv_sem=recvs.at[i, pair],
            device_id=worker(frame + 1, y), device_id_type=MESH,
        )

    def own_pair(arrival, i, pair):
        arrival(i, 2 * pair).wait()
        arrival(i, 2 * pair + 1).wait()

    def pass_on(i, arrival, buf, size, sends, recvs):
        for step in PAIR_ORDER:
            pair = (y_hi + step) % 4
            own_pair(arrival, i, pair)
            pl.when(has_next)(lambda: forward(buf, i, pair, size, sends, recvs).start())

    def previous(i, buf, size, sends, recvs):
        @pl.when(has_prev)
        def _():
            for pair in range(4):
                forward(buf, i, pair, size, sends, recvs).wait_recv()

        if i == K:
            @pl.when(jnp.logical_not(has_prev))
            def _():
                half = 8 * size
                buf[pl.ds(half, half), :] = buf[pl.ds(0, half), :]

    def spread(buf, left_buf, right_buf, size):
        half = 8 * size
        left = left_lanes((half, 128))
        one = jnp.ones((), BF16)
        own = buf[pl.ds(0, half), :]
        left_buf[pl.ds(0, half), :] = jnp.where(left, own, one)
        right_buf[pl.ds(0, half), :] = jnp.where(left, one, own)

    def spread_previous(buf, left_buf, right_buf, size):
        half = 8 * size
        left = left_lanes((half, 128))
        one = jnp.ones((), BF16)

        @pl.when(has_prev)
        def _():
            before = buf[pl.ds(half, half), :]
            left_buf[pl.ds(half, half), :] = jnp.where(left, before, one)
            right_buf[pl.ds(half, half), :] = jnp.where(left, one, before)

        @pl.when(jnp.logical_not(has_prev))
        def _():
            left_buf[pl.ds(half, half), :] = jnp.zeros((half, 128), BF16)
            right_buf[pl.ds(half, half), :] = jnp.zeros((half, 128), BF16)

    def weights(scores):
        return jnp.exp(scores - jnp.max(scores, axis=1, keepdims=True)).astype(BF16)

    scale = jnp.asarray(0.125, BF16)
    zero = jnp.zeros((), BF16)

    def o_tile(shard):
        return pltpu.make_async_remote_copy(
            src_ref=ot.at[rows_of(shard, ROWS)], dst_ref=ort.at[rows_of(y, ROWS)],
            send_sem=o_send_t.at[shard], recv_sem=o_recv_t.at[y],
            device_id=(frame, shard), device_id_type=MESH,
        )

    def o_head(shard):
        return pltpu.make_async_remote_copy(
            src_ref=oh.at[rows_of(shard, HALF)], dst_ref=orh.at[rows_of(y, HALF)],
            send_sem=o_send_h.at[shard], recv_sem=o_recv_h.at[y],
            device_id=(frame, shard), device_id_type=MESH,
        )

    def o_out(make, buf, back, size, recvs, pair):
        for shard in (2 * pair, 2 * pair + 1):
            own = owns & (space == shard)
            @pl.when(own)
            def _():
                pltpu.make_async_copy(buf.at[rows_of(shard, size)], back.at[rows_of(y, size)], recvs.at[y]).start()
            @pl.when(jnp.logical_not(own))
            def _():
                make(shard).start()

    def attend_tile(pair):
        own_pair(arrival_tile, Q, pair)
        q = qt[rows_of(pair, 2 * ROWS), :] * scale
        left = left_lanes(q.shape)
        a = jnp.dot(weights(dot_nt(jnp.where(left, q, zero), kt[...])), va[...], preferred_element_type=F32)
        b = jnp.dot(weights(dot_nt(jnp.where(left, zero, q), kt[...])), vb[...], preferred_element_type=F32)
        top = jnp.where(left, a, b)
        total = pltpu.roll(jnp.where(left, b, a), HALF, 1)
        ot[rows_of(pair, 2 * ROWS), :] = (top / total).astype(BF16)
        o_out(o_tile, ot, ort, ROWS, o_recv_t, pair)

    def attend_head(pair):
        own_pair(arrival_head, Q, pair)
        q = qh[rows_of(pair, 2 * HALF), :] * scale
        turned = swap_halves(q)
        left = left_lanes(q.shape)
        q_left = jnp.concatenate([jnp.where(left, q, zero), jnp.where(left, turned, zero)], 0)
        q_right = jnp.concatenate([jnp.where(left, zero, turned), jnp.where(left, zero, q)], 0)
        keys = kh[...]
        w = weights(jnp.concatenate([dot_nt(q_left, keys), dot_nt(q_right, keys)], 1))
        a = jnp.dot(w[:, :1024], ha[...], preferred_element_type=F32)
        b = jnp.dot(w[:, 1024:], hb[...], preferred_element_type=F32)
        both = a + pltpu.roll(b, HALF, 1)
        mixed = both / pltpu.roll(both, HALF, 1)
        oh[rows_of(pair, 2 * HALF), :] = jnp.where(
            left, mixed[:ROWS], pltpu.roll(mixed[ROWS:], HALF, 1)
        ).astype(BF16)
        o_out(o_head, oh, orh, HALF, o_recv_h, pair)

    def shifted(tile):
        return pltpu.make_async_remote_copy(
            src_ref=den_ref.at[0, :, columns(tile)], dst_ref=next_ref.at[0, :, columns(tile)],
            send_sem=shift_send.at[tile], recv_sem=shift_recv.at[tile],
            device_id=(queue - 1, space), device_id_type=MESH,
        )

    with jax.named_scope("wait_k"):
        pass_on(K, arrival_tile, kt, ROWS, fwd_send_t, fwd_recv_t)
    with jax.named_scope("wait_v"):
        pass_on(V, arrival_tile, vt, ROWS, fwd_send_t, fwd_recv_t)
    spread(vt, va, vb, ROWS)
    with jax.named_scope("wait_prev"):
        previous(K, kt, ROWS, fwd_send_t, fwd_recv_t)
        previous(V, vt, ROWS, fwd_send_t, fwd_recv_t)
    spread_previous(vt, va, vb, ROWS)
    for n, step in enumerate(PAIR_ORDER):
        with jax.named_scope("attend_tile"):
            attend_tile((y_hi + step) % 4)
        if n == 1:
            with jax.named_scope("wait_kh"):
                pass_on(K, arrival_head, kh, HALF, fwd_send_h, fwd_recv_h)
        if n == 2:
            with jax.named_scope("wait_vh"):
                pass_on(V, arrival_head, vh, HALF, fwd_send_h, fwd_recv_h)
    with jax.named_scope("wait_prev_h"):
        spread(vh, ha, hb, HALF)
        previous(K, kh, HALF, fwd_send_h, fwd_recv_h)
        previous(V, vh, HALF, fwd_send_h, fwd_recv_h)
        spread_previous(vh, ha, hb, HALF)

    gate_load.wait()
    step_now = plan_ref[levels_ref[0]]
    gate = gate_buf[pl.ds(step_now, 1), :]

    def gated(tile, attn):
        cut = slice(tile * 128, tile * 128 + 128)
        den_ref[0, :, cut] = (gate[:, cut] * attn.astype(F32)).astype(BF16)
        pl.when(has_ahead)(lambda: shifted(tile).start())

    def finish_tiles():
        for group in range(GROUPS):
            pltpu.make_async_copy(ort.at[pl.ds(0, ROWS)], ort.at[pl.ds(0, ROWS)], o_recv_t.at[group]).wait()
            gated(tile_of(group), ort[group * ROWS : (group + 1) * ROWS, :])

    def finish_heads():
        left = left_lanes((HALF, 128))
        for pair in range(4):
            for group in (2 * pair, 2 * pair + 1):
                pltpu.make_async_copy(orh.at[pl.ds(0, HALF)], orh.at[pl.ds(0, HALF)], o_recv_h.at[group]).wait()
            even = orh[2 * pair * HALF : (2 * pair + 1) * HALF, :]
            odd = orh[(2 * pair + 1) * HALF : (2 * pair + 2) * HALF, :]
            gated(
                3 * pair + 1,
                jnp.concatenate(
                    [jnp.where(left, even, swap_halves(odd)), jnp.where(left, swap_halves(even), odd)], 0
                ),
            )

    for n, step in enumerate(PAIR_ORDER):
        with jax.named_scope("attend_head"):
            attend_head((y_hi + step) % 4)
        if n == 2:
            with jax.named_scope("finish_tiles"):
                finish_tiles()
    with jax.named_scope("finish_heads"):
        finish_heads()

    @pl.when(jnp.logical_not(has_behind))
    def _():
        copy = pltpu.make_async_copy(fresh_hbm, next_ref.at[0], fresh_sem)
        copy.start()
        copy.wait()

    with jax.named_scope("wait_shift"):
        @pl.when(has_behind)
        def _():
            for tile in range(12):
                shifted(tile).wait_recv()

    with jax.named_scope("wait_sends"):
        @pl.when(has_ahead)
        def _():
            for tile in range(12):
                shifted(tile).wait_send()

        @pl.when(has_next)
        def _():
            for pair in range(4):
                for i, tiles, heads in ((K, kt, kh), (V, vt, vh)):
                    forward(tiles, i, pair, ROWS, fwd_send_t, fwd_recv_t).wait_send()
                    forward(heads, i, pair, HALF, fwd_send_h, fwd_recv_h).wait_send()

        for group in range(GROUPS):
            @pl.when(jnp.logical_not(owns & (group == y)))
            def _():
                for i in (K, V, Q):
                    sent_tile(i, group).wait_send()
                    sent_head(i, group).wait_send()

        for shard in range(8):
            @pl.when(jnp.logical_not(owns & (space == shard)))
            def _():
                o_tile(shard).wait_send()
                o_head(shard).wait_send()


def body(queries, keys, values, levels, plan, gate_table, fresh):
    vmem = functools.partial(pltpu.VMEM, dtype=BF16)
    dma = lambda *shape: pltpu.SemaphoreType.DMA(shape)
    any_space = pl.BlockSpec(memory_space=pl.ANY)
    smem = pl.BlockSpec(memory_space=pltpu.SMEM)
    out = jax.ShapeDtypeStruct((1, ROWS, COLS), BF16)
    return pl.pallas_call(
        kernel,
        out_shape=(out, out),
        in_specs=[any_space, any_space, any_space, smem, smem, any_space, any_space],
        out_specs=[pl.BlockSpec(memory_space=pltpu.VMEM)] * 2,
        scratch_shapes=[
            vmem((3, ROWS, COLS)), vmem((3, GROUPS, HALF, 128)), pltpu.VMEM((128, COLS), F32),
            vmem((2048, 128)), vmem((2048, 128)), vmem((1024, 128)),
            vmem((1024, 128)), vmem((1024, 128)), vmem((512, 128)),
            vmem((2048, 128)), vmem((2048, 128)), vmem((1024, 128)), vmem((1024, 128)),
            vmem((1024, 128)), vmem((512, 128)), vmem((1024, 128)), vmem((512, 128)),
            dma(3), pltpu.SemaphoreType.DMA,
            dma(3, 8), dma(3, 8), dma(3, 8), dma(3, 8),
            dma(2, 4), dma(2, 4), dma(2, 4), dma(2, 4),
            dma(8), dma(8), dma(8), dma(8),
            dma(12), dma(12), pltpu.SemaphoreType.DMA,
        ],
        compiler_params=pltpu.CompilerParams(
            collective_id=0, has_side_effects=True, vmem_limit_bytes=48 * 1024 * 1024
        ),
        name="frame_attention",
    )(queries, keys, values, levels, plan, gate_table, fresh)


def solution(mesh):
    return jax.shard_map(
        body,
        mesh=mesh,
        in_specs=(
            P("queue", "space", None),
            P("queue", "space", None),
            P("queue", "space", None),
            P("queue"),
            P(),
            P(),
            P("space", None),
        ),
        out_specs=(P("queue", "space", None), P("queue", "space", None)),
        check_vma=False,
    )
```

time: 136 us -> 67.1 us (0.49)
  the two profiles are of different devices: /device:TPU:136 before, /device:TPU:207 now
where the time goes in v1:
time: 67.1 us; the launch traced here: 66.8 us
  Pallas kernels  58.9 us (88%)
  local copies, waits for them, and re-layouts  6.61 us (10%)
  between operations  1.33 us (2%)
    pallas_call x1, Pallas kernels, body(): pl.pallas_call(kernel, out_shape=(out, out), in_specs=[any_space, any_spa...  58.9 us
    unnamed x14, local copies, waits for them, and re-layouts  6.61 us

profile of v1, /device:TPU:207, one launch (start us, length us, event | category | flops | bytes accessed | tf_op | source)
XLA Modules:
  0.0 66.8 jit_solution(6460396026372162692)
XLA Ops:
  0.6 0.0 copy-start.5
  1.3 0.0 copy-done.5
  1.3 0.0 copy-start
  1.3 1.1 %copy-done = f32[128,1536]{1,0:T(8,128)S(1)} copy-done((f32[128,1536]{1,0:T(8,128)S(1)}, f32[128,1536]{1,0:T(8,128)}, u32[]{:S(2)}) %copy-start) | copy-done | bytes 786456
  2.4 0.0 copy-start.1
  2.4 1.0 %copy-done.1 = bf16[1,128,1536]{2,1,0:T(8,128)(2,1)S(1)} copy-done((bf16[1,128,1536]{2,1,0:T(8,128)(2,1)S(1)}, bf16[1,128,1536]{2,1,0:T(8,128)(2,1)}, u32[]{:S(2)}) %copy-start.1) | copy-done | bytes 393240
  3.4 0.0 copy-start.2
  3.4 1.0 %copy-done.2 = bf16[1,128,1536]{2,1,0:T(8,128)(2,1)S(1)} copy-done((bf16[1,128,1536]{2,1,0:T(8,128)(2,1)S(1)}, bf16[1,128,1536]{2,1,0:T(8,128)(2,1)}, u32[]{:S(2)}) %copy-start.2) | copy-done | bytes 393240
  4.4 0.0 copy-start.3
  4.4 1.0 %copy-done.3 = bf16[1,128,1536]{2,1,0:T(8,128)(2,1)S(1)} copy-done((bf16[1,128,1536]{2,1,0:T(8,128)(2,1)S(1)}, bf16[1,128,1536]{2,1,0:T(8,128)(2,1)}, u32[]{:S(2)}) %copy-start.3) | copy-done | bytes 393240
  5.4 0.0 copy-start.4
  5.4 1.0 %copy-done.4 = bf16[128,1536]{1,0:T(8,128)(2,1)S(1)} copy-done((bf16[128,1536]{1,0:T(8,128)(2,1)S(1)}, bf16[128,1536]{1,0:T(8,128)(2,1)}, u32[]{:S(2)}) %copy-start.4) | copy-done | bytes 393240
  6.4 58.9 %frame_attention.1 = (bf16[1,128,1536]{2,1,0:T(8,128)(2,1)S(1)}, bf16[1,128,1536]{2,1,0:T(8,128)(2,1)S(1)}) custom-call(bf16[1,128,1536]{2,1,0:T(8,128)(2,1)S(1)} %copy-done.1, bf16[1,128,1536]{2,1,0:T(8,128)(2,1)S(1)} %copy-done.2, bf16[1,128,1536]{2,1,0:T(8,128)(2,1)S(1)} %copy-done.3, s32[1]{0:T(128)S(6)} %copy.11.levels_ref, s32[64]{0:T(128)S(1)} %copy-done.5, ...), custom_call_target="tpu_custom_call" | custom-call | tf_op jit(solution)/shard_map/frame_attention/pallas_call | solution.py:401
  65.3 0.7 %copy.12 = bf16[1,128,1536]{2,1,0:T(8,128)(2,1)} copy(bf16[1,128,1536]{2,1,0:T(8,128)(2,1)S(1)} %get-tuple-element.4) | data formatting | bytes 786432
  66.0 0.7 %copy.13 = bf16[1,128,1536]{2,1,0:T(8,128)(2,1)} copy(bf16[1,128,1536]{2,1,0:T(8,128)(2,1)S(1)} %get-tuple-element.5) | data formatting | bytes 786432
Async XLA Ops:
  0.6 0.7 %copy-start.5 = (s32[64]{0:T(128)S(1)}, s32[64]{0:T(128)}, u32[]{:S(2)}) copy-start(s32[64]{0:T(128)} %plan_ref.1) | copy-start | bytes 772
  1.3 1.1 %copy-start = (f32[128,1536]{1,0:T(8,128)S(1)}, f32[128,1536]{1,0:T(8,128)}, u32[]{:S(2)}) copy-start(f32[128,1536]{1,0:T(8,128)} %gate_hbm.1) | copy-start | bytes 2359300
  2.4 1.0 %copy-start.1 = (bf16[1,128,1536]{2,1,0:T(8,128)(2,1)S(1)}, bf16[1,128,1536]{2,1,0:T(8,128)(2,1)}, u32[]{:S(2)}) copy-start(bf16[1,128,1536]{2,1,0:T(8,128)(2,1)} %q_hbm.1) | copy-start | bytes 1179652
  3.4 1.0 %copy-start.2 = (bf16[1,128,1536]{2,1,0:T(8,128)(2,1)S(1)}, bf16[1,128,1536]{2,1,0:T(8,128)(2,1)}, u32[]{:S(2)}) copy-start(bf16[1,128,1536]{2,1,0:T(8,128)(2,1)} %k_hbm.1) | copy-start | bytes 1179652
  4.4 1.0 %copy-start.3 = (bf16[1,128,1536]{2,1,0:T(8,128)(2,1)S(1)}, bf16[1,128,1536]{2,1,0:T(8,128)(2,1)}, u32[]{:S(2)}) copy-start(bf16[1,128,1536]{2,1,0:T(8,128)(2,1)} %v_hbm.1) | copy-start | bytes 1179652
  5.4 1.0 %copy-start.4 = (bf16[128,1536]{1,0:T(8,128)(2,1)S(1)}, bf16[128,1536]{1,0:T(8,128)(2,1)}, u32[]{:S(2)}) copy-start(bf16[128,1536]{1,0:T(8,128)(2,1)} %fresh_hbm.1) | copy-start | bytes 1179652

commit v2 on v1

--- a/solution.py
+++ b/solution.py
@@ -14,8 +14,7 @@
 HALF = 64
 COLS = 1536
 GROUPS = 8
-FAR_FIRST = (4, 3, 5, 2, 6, 1, 7, 0)
-PAIR_ORDER = (2, 1, 3, 0)
+NEAR_FIRST = (0, 1, 7, 2, 6, 3, 5, 4)
 K, V, Q = 0, 1, 2
 
 
@@ -42,7 +41,7 @@
 def kernel(
     q_hbm, k_hbm, v_hbm, levels_ref, plan_ref, gate_hbm, fresh_hbm,
     den_ref, next_ref,
-    src, packed, gate_buf,
+    src, packed, gate_buf, gate_row,
     kt, vt, qt, kh, vh, qh,
     va, vb, ha, hb,
     ot, oh, ort, orh,
@@ -58,6 +57,8 @@
     y_hi, core = space // 2, space % 2
     y = y_hi * 2 + y_lo
     frame = z * 8 + core * 4 + x
+    nearer = 3 - 2 * y_lo
+    near_pairs = [(y_hi + step) % 4 for step in (0, nearer, 4 - nearer, 2)]
     tokens_in = (kt, vt, qt)
     heads_in = (kh, vh, qh)
 
@@ -67,14 +68,11 @@
             (group // 2) * 2 + (of_frame // 4) % 2,
         )
 
+    inputs = (k_hbm, v_hbm, q_hbm)
     loads = [
-        pltpu.make_async_copy(ref.at[0], src.at[i], in_sem.at[i])
-        for i, ref in enumerate((k_hbm, v_hbm, q_hbm))
+        pltpu.make_async_copy(ref.at[0], src.at[i], in_sem.at[i]) for i, ref in enumerate(inputs)
     ]
-    for load in loads:
-        load.start()
     gate_load = pltpu.make_async_copy(gate_hbm, gate_buf, gate_sem)
-    gate_load.start()
 
     barrier = pltpu.get_barrier_semaphore()
 
@@ -109,9 +107,9 @@
             packed[i, 2 * pair] = jnp.where(left, top, swap_halves(bottom))
             packed[i, 2 * pair + 1] = jnp.where(left, swap_halves(top), bottom)
 
-    for i in (K, V, Q):
-        loads[i].wait()
-        pack(i)
+    for load in loads:
+        load.start()
+    gate_load.start()
     pl.semaphore_wait(barrier, greeted)
 
     def rows_of(index, size):
@@ -134,7 +132,7 @@
         )
 
     def send_out(make, kept, i):
-        for shift in FAR_FIRST:
+        for shift in NEAR_FIRST:
             group = (y + shift) % GROUPS
             if shift:
                 make(i, group).start()
@@ -158,8 +156,10 @@
 
     with jax.named_scope("send_all"):
         for i in (K, V, Q):
+            loads[i].wait()
             send_out(sent_tile, kept_tile, i)
-        for i in (K, V, Q):
+            pack(i)
+        for i in (K, V):
             send_out(sent_head, kept_head, i)
 
     def arrival_tile(i, shard):
@@ -185,8 +185,7 @@
         arrival(i, 2 * pair + 1).wait()
 
     def pass_on(i, arrival, buf, size, sends, recvs):
-        for step in PAIR_ORDER:
-            pair = (y_hi + step) % 4
+        for pair in near_pairs:
             own_pair(arrival, i, pair)
             pl.when(has_next)(lambda: forward(buf, i, pair, size, sends, recvs).start())
 
@@ -301,58 +300,68 @@
         previous(K, kt, ROWS, fwd_send_t, fwd_recv_t)
         previous(V, vt, ROWS, fwd_send_t, fwd_recv_t)
     spread_previous(vt, va, vb, ROWS)
-    for n, step in enumerate(PAIR_ORDER):
+    for n, pair in enumerate(near_pairs):
         with jax.named_scope("attend_tile"):
-            attend_tile((y_hi + step) % 4)
+            attend_tile(pair)
+        if n == 1:
+            send_out(sent_head, kept_head, Q)
         if n == 1:
             with jax.named_scope("wait_kh"):
                 pass_on(K, arrival_head, kh, HALF, fwd_send_h, fwd_recv_h)
         if n == 2:
             with jax.named_scope("wait_vh"):
                 pass_on(V, arrival_head, vh, HALF, fwd_send_h, fwd_recv_h)
+
+    gate_load.wait()
+    step_now = plan_ref[levels_ref[0]]
+    gate_row[...] = gate_buf[pl.ds(step_now, 1), :]
+
+    def gated(tile, attn):
+        cut = columns(tile)
+        den_ref[0, :, cut] = (gate_row[:, cut] * attn.astype(F32)).astype(BF16)
+        pl.when(has_ahead)(lambda: shifted(tile).start())
+
+    def arrived(back, index, size, recvs):
+        pltpu.make_async_copy(
+            back.at[rows_of(index, size)], back.at[rows_of(index, size)], recvs.at[index]
+        ).wait()
+
+    def finish_tile(group):
+        arrived(ort, group, ROWS, o_recv_t)
+        gated(tile_of(group), ort[rows_of(group, ROWS), :])
+
+    def finish_heads(pair):
+        left = left_lanes((HALF, 128))
+        for group in (2 * pair, 2 * pair + 1):
+            arrived(orh, group, HALF, o_recv_h)
+        even = orh[rows_of(2 * pair, HALF), :]
+        odd = orh[rows_of(2 * pair + 1, HALF), :]
+        gated(
+            3 * pair + 1,
+            jnp.concatenate(
+                [jnp.where(left, even, swap_halves(odd)), jnp.where(left, swap_halves(even), odd)], 0
+            ),
+        )
+
     with jax.named_scope("wait_prev_h"):
         spread(vh, ha, hb, HALF)
         previous(K, kh, HALF, fwd_send_h, fwd_recv_h)
         previous(V, vh, HALF, fwd_send_h, fwd_recv_h)
         spread_previous(vh, ha, hb, HALF)
 
-    gate_load.wait()
-    step_now = plan_ref[levels_ref[0]]
-    gate = gate_buf[pl.ds(step_now, 1), :]
-
-    def gated(tile, attn):
-        cut = slice(tile * 128, tile * 128 + 128)
-        den_ref[0, :, cut] = (gate[:, cut] * attn.astype(F32)).astype(BF16)
-        pl.when(has_ahead)(lambda: shifted(tile).start())
-
-    def finish_tiles():
-        for group in range(GROUPS):
-            pltpu.make_async_copy(ort.at[pl.ds(0, ROWS)], ort.at[pl.ds(0, ROWS)], o_recv_t.at[group]).wait()
-            gated(tile_of(group), ort[group * ROWS : (group + 1) * ROWS, :])
-
-    def finish_heads():
-        left = left_lanes((HALF, 128))
-        for pair in range(4):
-            for group in (2 * pair, 2 * pair + 1):
-                pltpu.make_async_copy(orh.at[pl.ds(0, HALF)], orh.at[pl.ds(0, HALF)], o_recv_h.at[group]).wait()
-            even = orh[2 * pair * HALF : (2 * pair + 1) * HALF, :]
-            odd = orh[(2 * pair + 1) * HALF : (2 * pair + 2) * HALF, :]
-            gated(
-                3 * pair + 1,
-                jnp.concatenate(
-                    [jnp.where(left, even, swap_halves(odd)), jnp.where(left, swap_halves(even), odd)], 0
-                ),
-            )
-
-    for n, step in enumerate(PAIR_ORDER):
+    home = [(y_hi + step) % 4 for step in (0, 1, 3, 2)]
+    tile_groups = [2 * home[0], 2 * home[0] + 1, 2 * home[1], 2 * home[2] + 1,
+                   2 * home[2], 2 * home[1] + 1, 2 * home[3], 2 * home[3] + 1]
+    for group in tile_groups[:4]:
+        finish_tile(group)
+    for n, pair in enumerate(near_pairs):
         with jax.named_scope("attend_head"):
-            attend_head((y_hi + step) % 4)
-        if n == 2:
-            with jax.named_scope("finish_tiles"):
-                finish_tiles()
-    with jax.named_scope("finish_heads"):
-        finish_heads()
-
+            attend_head(pair)
+    with jax.named_scope("finish"):
+        for group in tile_groups[4:]:
+            finish_tile(group)
+        for pair in home:
+            finish_heads(pair)
     @pl.when(jnp.logical_not(has_behind))
     def _():
         copy = pltpu.make_async_copy(fresh_hbm, next_ref.at[0], fresh_sem)
@@ -392,19 +401,30 @@
                 o_head(shard).wait_send()
 
 
+def hand_over(den_ref, next_ref, den_out, next_out, sems):
+    copies = [
+        pltpu.make_async_copy(den_ref, den_out, sems.at[0]),
+        pltpu.make_async_copy(next_ref, next_out, sems.at[1]),
+    ]
+    for copy in copies:
+        copy.start()
+    for copy in copies:
+        copy.wait()
+
+
 def body(queries, keys, values, levels, plan, gate_table, fresh):
     vmem = functools.partial(pltpu.VMEM, dtype=BF16)
     dma = lambda *shape: pltpu.SemaphoreType.DMA(shape)
     any_space = pl.BlockSpec(memory_space=pl.ANY)
     smem = pl.BlockSpec(memory_space=pltpu.SMEM)
     out = jax.ShapeDtypeStruct((1, ROWS, COLS), BF16)
-    return pl.pallas_call(
+    results = pl.pallas_call(
         kernel,
         out_shape=(out, out),
         in_specs=[any_space, any_space, any_space, smem, smem, any_space, any_space],
         out_specs=[pl.BlockSpec(memory_space=pltpu.VMEM)] * 2,
         scratch_shapes=[
-            vmem((3, ROWS, COLS)), vmem((3, GROUPS, HALF, 128)), pltpu.VMEM((128, COLS), F32),
+            vmem((3, ROWS, COLS)), vmem((3, GROUPS, HALF, 128)), pltpu.VMEM((128, COLS), F32), pltpu.VMEM((1, COLS), F32),
             vmem((2048, 128)), vmem((2048, 128)), vmem((1024, 128)),
             vmem((1024, 128)), vmem((1024, 128)), vmem((512, 128)),
             vmem((2048, 128)), vmem((2048, 128)), vmem((1024, 128)), vmem((1024, 128)),
@@ -416,10 +436,19 @@
             dma(12), dma(12), pltpu.SemaphoreType.DMA,
         ],
         compiler_params=pltpu.CompilerParams(
-            collective_id=0, has_side_effects=True, vmem_limit_bytes=48 * 1024 * 1024
+            collective_id=0, has_side_effects=True, vmem_limit_bytes=53 * 1024 * 1024
         ),
         name="frame_attention",
     )(queries, keys, values, levels, plan, gate_table, fresh)
+    return pl.pallas_call(
+        hand_over,
+        out_shape=(out, out),
+        in_specs=[pl.BlockSpec(memory_space=pl.ANY)] * 2,
+        out_specs=[pl.BlockSpec(memory_space=pl.ANY)] * 2,
+        scratch_shapes=[dma(2)],
+        compiler_params=pltpu.CompilerParams(vmem_limit_bytes=8 * 1024 * 1024),
+        name="hand_over",
+    )(*results)
 
 
 def solution(mesh):

time: 67.1 us -> 57.8 us (0.86)
  local copies, waits for them, and re-layouts: 6.61 us -> 0.01 us
  Pallas kernels: 58.9 us -> 56.3 us
    unnamed x14 -> x2, local copies, waits for them, and re-layouts: 6.61 us -> 0.01 us
    pallas_call x1, Pallas kernels: 58.9 us -> 55.4 us  [body(): pl.pallas_call(kernel, out_shape=(out, out), in_specs=[any_space, any_spa...]
    pallas_call x0 -> x1, Pallas kernels: none -> 0.89 us  [body(): pl.pallas_call(hand_over, out_shape=(out, out), in_specs=[pl.BlockSpec(me...]
where the time goes in v2:
time: 57.8 us; the launch traced here: 57.6 us
  Pallas kernels  56.3 us (97%)
  between operations  1.31 us (2%)
    pallas_call x1, Pallas kernels, body(): pl.pallas_call(kernel, out_shape=(out, out), in_specs=[any_space, any_spa...  55.4 us

profile of v2, /device:TPU:207, one launch (start us, length us, event | category | flops | bytes accessed | tf_op | source)
XLA Modules:
  0.0 57.6 jit_solution(4231734824490561208)
XLA Ops:
  0.6 0.0 copy-start
  1.3 0.0 copy-done
  1.3 55.4 %frame_attention.1 = (bf16[1,128,1536]{2,1,0:T(8,128)(2,1)S(1)}, bf16[1,128,1536]{2,1,0:T(8,128)(2,1)S(1)}) custom-call(bf16[1,128,1536]{2,1,0:T(8,128)(2,1)} %q_hbm.1, bf16[1,128,1536]{2,1,0:T(8,128)(2,1)} %k_hbm.1, bf16[1,128,1536]{2,1,0:T(8,128)(2,1)} %v_hbm.1, s32[1]{0:T(128)S(6)} %copy.9.levels_ref, s32[64]{0:T(128)S(1)} %copy-done, ...), custom_call_target="tpu_custom_call" | custom-call | tf_op jit(solution)/shard_map/frame_attention/pallas_call | solution.py:421
  56.7 0.9 %hand_over.1 = (bf16[1,128,1536]{2,1,0:T(8,128)(2,1)}, bf16[1,128,1536]{2,1,0:T(8,128)(2,1)}) custom-call(bf16[1,128,1536]{2,1,0:T(8,128)(2,1)S(1)} %get-tuple-element.4.den_ref, bf16[1,128,1536]{2,1,0:T(8,128)(2,1)S(1)} %get-tuple-element.5.next_ref), custom_call_target="tpu_custom_call" | custom-call | tf_op jit(solution)/shard_map/hand_over/pallas_call | solution.py:443
Async XLA Ops:
  0.6 0.7 %copy-start = (s32[64]{0:T(128)S(1)}, s32[64]{0:T(128)}, u32[]{:S(2)}) copy-start(s32[64]{0:T(128)} %plan_ref.1) | copy-start | bytes 772

commit v3 on v2

--- a/solution.py
+++ b/solution.py
@@ -16,6 +16,7 @@
 GROUPS = 8
 NEAR_FIRST = (0, 1, 7, 2, 6, 3, 5, 4)
 K, V, Q = 0, 1, 2
+VIA = (3, 1, 2, 3)
 
 
 def dot_nt(a, b):
@@ -39,8 +40,9 @@
 
 
 def kernel(
-    q_hbm, k_hbm, v_hbm, levels_ref, plan_ref, gate_hbm, fresh_hbm,
+    q_hbm, k_hbm, v_hbm, levels_hbm, plan_hbm, gate_hbm, fresh_hbm,
     den_ref, next_ref,
+    levels_ref, plan_ref, index_sem,
     src, packed, gate_buf, gate_row,
     kt, vt, qt, kh, vh, qh,
     va, vb, ha, hb,
@@ -50,6 +52,7 @@
     fwd_send_t, fwd_recv_t, fwd_send_h, fwd_recv_h,
     o_send_t, o_recv_t, o_send_h, o_recv_h,
     shift_send, shift_recv, fresh_sem,
+    relay_buf, relay_send, relay_recv,
 ):
     queue = lax.axis_index("queue")
     space = lax.axis_index("space")
@@ -74,6 +77,16 @@
     ]
     gate_load = pltpu.make_async_copy(gate_hbm, gate_buf, gate_sem)
 
+    for load in loads:
+        load.start()
+    gate_load.start()
+    index_loads = [
+        pltpu.make_async_copy(levels_hbm, levels_ref, index_sem.at[0]),
+        pltpu.make_async_copy(plan_hbm, plan_ref, index_sem.at[1]),
+    ]
+    for load in index_loads:
+        load.start()
+
     barrier = pltpu.get_barrier_semaphore()
 
     def greet(device):
@@ -81,6 +94,8 @@
 
     has_prev, has_next = frame > 0, frame < 63
     has_ahead, has_behind = queue > 0, queue < 63
+    wraps = has_ahead & (x == 0)
+    relays = (x > 0) & (queue - x > 0)
     owns = core == y_lo
     for i in range(8):
         @pl.when(jnp.logical_not(owns & (space == i)))
@@ -88,6 +103,14 @@
             greet((frame, i))
     pl.when(has_prev)(lambda: greet(worker(frame - 1, y)))
     pl.when(has_behind)(lambda: greet((queue + 1, space)))
+
+    @pl.when(has_behind & (x == 3))
+    def _():
+        for column in sorted(set(VIA)):
+            greet((queue + 1 + column, space))
+
+    for column in sorted(set(VIA)):
+        pl.when(relays & (x == column))(lambda: greet((queue - x, space)))
     for i in range(GROUPS):
         @pl.when(jnp.logical_not(owns & (y == i)))
         def _():
@@ -97,6 +120,8 @@
         - 2 * owns.astype(jnp.int32)
         + has_next.astype(jnp.int32)
         + has_ahead.astype(jnp.int32)
+        + len(set(VIA)) * wraps.astype(jnp.int32)
+        + sum((relays & (x == column)).astype(jnp.int32) for column in sorted(set(VIA)))
     )
 
     def pack(i):
@@ -107,9 +132,6 @@
             packed[i, 2 * pair] = jnp.where(left, top, swap_halves(bottom))
             packed[i, 2 * pair + 1] = jnp.where(left, swap_halves(top), bottom)
 
-    for load in loads:
-        load.start()
-    gate_load.start()
     pl.semaphore_wait(barrier, greeted)
 
     def rows_of(index, size):
@@ -131,8 +153,8 @@
             device_id=worker(queue, group), device_id_type=MESH,
         )
 
-    def send_out(make, kept, i):
-        for shift in NEAR_FIRST:
+    def send_out(make, kept, i, order=NEAR_FIRST):
+        for shift in order:
             group = (y + shift) % GROUPS
             if shift:
                 make(i, group).start()
@@ -291,6 +313,20 @@
             device_id=(queue - 1, space), device_id_type=MESH,
         )
 
+    def to_relay(tile, k):
+        return pltpu.make_async_remote_copy(
+            src_ref=den_ref.at[0, :, columns(tile)], dst_ref=relay_buf.at[k],
+            send_sem=shift_send.at[tile], recv_sem=relay_recv.at[k],
+            device_id=(queue + VIA[k], space), device_id_type=MESH,
+        )
+
+    def from_relay(tile, k):
+        return pltpu.make_async_remote_copy(
+            src_ref=relay_buf.at[k], dst_ref=next_ref.at[0, :, columns(tile)],
+            send_sem=relay_send.at[k], recv_sem=shift_recv.at[tile],
+            device_id=(queue - x - 1, space), device_id_type=MESH,
+        )
+
     with jax.named_scope("wait_k"):
         pass_on(K, arrival_tile, kt, ROWS, fwd_send_t, fwd_recv_t)
     with jax.named_scope("wait_v"):
@@ -303,8 +339,8 @@
     for n, pair in enumerate(near_pairs):
         with jax.named_scope("attend_tile"):
             attend_tile(pair)
-        if n == 1:
-            send_out(sent_head, kept_head, Q)
+        if n == 0:
+            send_out(sent_head, kept_head, Q, NEAR_FIRST[::-1])
         if n == 1:
             with jax.named_scope("wait_kh"):
                 pass_on(K, arrival_head, kh, HALF, fwd_send_h, fwd_recv_h)
@@ -313,22 +349,44 @@
                 pass_on(V, arrival_head, vh, HALF, fwd_send_h, fwd_recv_h)
 
     gate_load.wait()
+    for load in index_loads:
+        load.wait()
     step_now = plan_ref[levels_ref[0]]
     gate_row[...] = gate_buf[pl.ds(step_now, 1), :]
 
-    def gated(tile, attn):
+    def gated(tile, attn, k=len(VIA)):
         cut = columns(tile)
         den_ref[0, :, cut] = (gate_row[:, cut] * attn.astype(F32)).astype(BF16)
-        pl.when(has_ahead)(lambda: shifted(tile).start())
+        if k < len(VIA):
+            pl.when(has_ahead & (x > 0))(lambda: shifted(tile).start())
+            pl.when(wraps)(lambda: to_relay(tile, k).start())
+        else:
+            pl.when(has_ahead)(lambda: shifted(tile).start())
 
     def arrived(back, index, size, recvs):
         pltpu.make_async_copy(
             back.at[rows_of(index, size)], back.at[rows_of(index, size)], recvs.at[index]
         ).wait()
 
-    def finish_tile(group):
+    def finish_tile(k):
+        group = tile_groups[k]
         arrived(ort, group, ROWS, o_recv_t)
-        gated(tile_of(group), ort[rows_of(group, ROWS), :])
+        gated(tile_of(group), ort[rows_of(group, ROWS), :], k)
+
+    def relay(act):
+        for column in sorted(set(VIA)):
+            @pl.when(relays & (x == column))
+            def _():
+                for k in range(len(VIA)):
+                    if VIA[k] == column:
+                        act(k)
+
+    def pass_relayed(k):
+        pltpu.make_async_copy(relay_buf.at[k], relay_buf.at[k], relay_recv.at[k]).wait()
+        from_relay(tile_of(tile_groups[k]), k).start()
+
+    def wait_relayed(k):
+        from_relay(tile_of(tile_groups[k]), k).wait_send()
 
     def finish_heads(pair):
         left = left_lanes((HALF, 128))
@@ -352,15 +410,34 @@
     home = [(y_hi + step) % 4 for step in (0, 1, 3, 2)]
     tile_groups = [2 * home[0], 2 * home[0] + 1, 2 * home[1], 2 * home[2] + 1,
                    2 * home[2], 2 * home[1] + 1, 2 * home[3], 2 * home[3] + 1]
-    for group in tile_groups[:4]:
-        finish_tile(group)
-    for n, pair in enumerate(near_pairs):
+    for k in range(4):
+        finish_tile(k)
+    for pair in near_pairs[::-1]:
         with jax.named_scope("attend_head"):
             attend_head(pair)
+    with jax.named_scope("sent"):
+        @pl.when(has_next)
+        def _():
+            for pair in range(4):
+                for i, tiles, heads in ((K, kt, kh), (V, vt, vh)):
+                    forward(tiles, i, pair, ROWS, fwd_send_t, fwd_recv_t).wait_send()
+                    forward(heads, i, pair, HALF, fwd_send_h, fwd_recv_h).wait_send()
+
+        for group in range(GROUPS):
+            @pl.when(jnp.logical_not(owns & (group == y)))
+            def _():
+                for i in (K, V, Q):
+                    sent_tile(i, group).wait_send()
+                    sent_head(i, group).wait_send()
     with jax.named_scope("finish"):
-        for group in tile_groups[4:]:
-            finish_tile(group)
-        for pair in home:
+        relay(pass_relayed)
+        for k in range(4, 8):
+            finish_tile(k)
+        for shard in range(8):
+            @pl.when(jnp.logical_not(owns & (space == shard)))
+            def _():
+                o_tile(shard).wait_send()
+        for pair in home[::-1]:
             finish_heads(pair)
     @pl.when(jnp.logical_not(has_behind))
     def _():
@@ -375,29 +452,16 @@
                 shifted(tile).wait_recv()
 
     with jax.named_scope("wait_sends"):
+        relay(wait_relayed)
+
         @pl.when(has_ahead)
         def _():
             for tile in range(12):
                 shifted(tile).wait_send()
 
-        @pl.when(has_next)
-        def _():
-            for pair in range(4):
-                for i, tiles, heads in ((K, kt, kh), (V, vt, vh)):
-                    forward(tiles, i, pair, ROWS, fwd_send_t, fwd_recv_t).wait_send()
-                    forward(heads, i, pair, HALF, fwd_send_h, fwd_recv_h).wait_send()
-
-        for group in range(GROUPS):
-            @pl.when(jnp.logical_not(owns & (group == y)))
-            def _():
-                for i in (K, V, Q):
-                    sent_tile(i, group).wait_send()
-                    sent_head(i, group).wait_send()
-
         for shard in range(8):
             @pl.when(jnp.logical_not(owns & (space == shard)))
             def _():
-                o_tile(shard).wait_send()
                 o_head(shard).wait_send()
 
 
@@ -416,14 +480,14 @@
     vmem = functools.partial(pltpu.VMEM, dtype=BF16)
     dma = lambda *shape: pltpu.SemaphoreType.DMA(shape)
     any_space = pl.BlockSpec(memory_space=pl.ANY)
-    smem = pl.BlockSpec(memory_space=pltpu.SMEM)
     out = jax.ShapeDtypeStruct((1, ROWS, COLS), BF16)
     results = pl.pallas_call(
         kernel,
         out_shape=(out, out),
-        in_specs=[any_space, any_space, any_space, smem, smem, any_space, any_space],
+        in_specs=[any_space] * 7,
         out_specs=[pl.BlockSpec(memory_space=pltpu.VMEM)] * 2,
         scratch_shapes=[
+            pltpu.SMEM((1,), jnp.int32), pltpu.SMEM((64,), jnp.int32), dma(2),
             vmem((3, ROWS, COLS)), vmem((3, GROUPS, HALF, 128)), pltpu.VMEM((128, COLS), F32), pltpu.VMEM((1, COLS), F32),
             vmem((2048, 128)), vmem((2048, 128)), vmem((1024, 128)),
             vmem((1024, 128)), vmem((1024, 128)), vmem((512, 128)),
@@ -434,6 +498,7 @@
             dma(2, 4), dma(2, 4), dma(2, 4), dma(2, 4),
             dma(8), dma(8), dma(8), dma(8),
             dma(12), dma(12), pltpu.SemaphoreType.DMA,
+            vmem((len(VIA), ROWS, 128)), dma(len(VIA)), dma(len(VIA)),
         ],
         compiler_params=pltpu.CompilerParams(
             collective_id=0, has_side_effects=True, vmem_limit_bytes=53 * 1024 * 1024

time: 57.8 us -> 56.6 us (0.979)
  Pallas kernels: 56.3 us -> 55.1 us
    pallas_call x1, Pallas kernels: 55.4 us -> 54.2 us  [body(): pl.pallas_call(kernel, out_shape=(out, out), in_specs=[any_space] * 7, ou...]
where the time goes in v3:
time: 56.6 us; the launch traced here: 56.4 us
  Pallas kernels  55.1 us (97%)
  between operations  1.31 us (2%)
    pallas_call x1, Pallas kernels, body(): pl.pallas_call(kernel, out_shape=(out, out), in_specs=[any_space] * 7, ou...  54.2 us

profile of v3, /device:TPU:207, one launch (start us, length us, event | category | flops | bytes accessed | tf_op | source)
XLA Modules:
  0.0 56.4 jit_solution(3691719091985112096)
XLA Ops:
  0.6 0.0 copy-start
  1.3 0.0 copy-done
  1.3 54.2 %frame_attention.1 = (bf16[1,128,1536]{2,1,0:T(8,128)(2,1)S(1)}, bf16[1,128,1536]{2,1,0:T(8,128)(2,1)S(1)}) custom-call(bf16[1,128,1536]{2,1,0:T(8,128)(2,1)} %q_hbm.1, bf16[1,128,1536]{2,1,0:T(8,128)(2,1)} %k_hbm.1, bf16[1,128,1536]{2,1,0:T(8,128)(2,1)} %v_hbm.1, s32[1]{0:T(128)S(6)} %copy.9.levels_hbm, s32[64]{0:T(128)S(1)} %copy-done, ...), custom_call_target="tpu_custom_call" | custom-call | tf_op jit(solution)/shard_map/frame_attention/pallas_call | solution.py:484
  55.5 0.9 %hand_over.1 = (bf16[1,128,1536]{2,1,0:T(8,128)(2,1)}, bf16[1,128,1536]{2,1,0:T(8,128)(2,1)}) custom-call(bf16[1,128,1536]{2,1,0:T(8,128)(2,1)S(1)} %get-tuple-element.4.den_ref, bf16[1,128,1536]{2,1,0:T(8,128)(2,1)S(1)} %get-tuple-element.5.next_ref), custom_call_target="tpu_custom_call" | custom-call | tf_op jit(solution)/shard_map/hand_over/pallas_call | solution.py:508
Async XLA Ops:
  0.6 0.7 %copy-start = (s32[64]{0:T(128)S(1)}, s32[64]{0:T(128)}, u32[]{:S(2)}) copy-start(s32[64]{0:T(128)} %plan_hbm.1) | copy-start | bytes 772

commit v4 on v3

--- a/solution.py
+++ b/solution.py
@@ -288,23 +288,26 @@
         ot[rows_of(pair, 2 * ROWS), :] = (top / total).astype(BF16)
         o_out(o_tile, ot, ort, ROWS, o_recv_t, pair)
 
-    def attend_head(pair):
-        own_pair(arrival_head, Q, pair)
-        q = qh[rows_of(pair, 2 * HALF), :] * scale
-        turned = swap_halves(q)
-        left = left_lanes(q.shape)
-        q_left = jnp.concatenate([jnp.where(left, q, zero), jnp.where(left, turned, zero)], 0)
-        q_right = jnp.concatenate([jnp.where(left, zero, turned), jnp.where(left, zero, q)], 0)
+    def attend_heads(pairs):
+        for pair in pairs:
+            own_pair(arrival_head, Q, pair)
         keys = kh[...]
-        w = weights(jnp.concatenate([dot_nt(q_left, keys), dot_nt(q_right, keys)], 1))
-        a = jnp.dot(w[:, :1024], ha[...], preferred_element_type=F32)
-        b = jnp.dot(w[:, 1024:], hb[...], preferred_element_type=F32)
-        both = a + pltpu.roll(b, HALF, 1)
-        mixed = both / pltpu.roll(both, HALF, 1)
-        oh[rows_of(pair, 2 * HALF), :] = jnp.where(
-            left, mixed[:ROWS], pltpu.roll(mixed[ROWS:], HALF, 1)
-        ).astype(BF16)
-        o_out(o_head, oh, orh, HALF, o_recv_h, pair)
+        for pair in pairs:
+            q = qh[rows_of(pair, 2 * HALF), :] * scale
+            turned = swap_halves(q)
+            left = left_lanes(q.shape)
+            q_left = jnp.concatenate([jnp.where(left, q, zero), jnp.where(left, turned, zero)], 0)
+            q_right = jnp.concatenate([jnp.where(left, zero, turned), jnp.where(left, zero, q)], 0)
+            w = weights(jnp.concatenate([dot_nt(q_left, keys), dot_nt(q_right, keys)], 1))
+            a = jnp.dot(w[:, :1024], ha[...], preferred_element_type=F32)
+            b = jnp.dot(w[:, 1024:], hb[...], preferred_element_type=F32)
+            both = a + pltpu.roll(b, HALF, 1)
+            mixed = both / pltpu.roll(both, HALF, 1)
+            oh[rows_of(pair, 2 * HALF), :] = jnp.where(
+                left, mixed[:ROWS], pltpu.roll(mixed[ROWS:], HALF, 1)
+            ).astype(BF16)
+        for pair in pairs:
+            o_out(o_head, oh, orh, HALF, o_recv_h, pair)
 
     def shifted(tile):
         return pltpu.make_async_remote_copy(
@@ -412,9 +415,9 @@
                    2 * home[2], 2 * home[1] + 1, 2 * home[3], 2 * home[3] + 1]
     for k in range(4):
         finish_tile(k)
-    for pair in near_pairs[::-1]:
+    for pairs in (near_pairs[:1:-1], near_pairs[1::-1]):
         with jax.named_scope("attend_head"):
-            attend_head(pair)
+            attend_heads(pairs)
     with jax.named_scope("sent"):
         @pl.when(has_next)
         def _():
@@ -484,7 +487,7 @@
     results = pl.pallas_call(
         kernel,
         out_shape=(out, out),
-        in_specs=[any_space] * 7,
+        in_specs=[any_space] * 3 + [pl.BlockSpec(memory_space=pltpu.HBM)] * 2 + [any_space] * 2,
         out_specs=[pl.BlockSpec(memory_space=pltpu.VMEM)] * 2,
         scratch_shapes=[
             pltpu.SMEM((1,), jnp.int32), pltpu.SMEM((64,), jnp.int32), dma(2),

time: 56.6 us -> 56.2 us (level)
  no operation moved by 1% of the time
where the time goes in v4:
time: 56.2 us; the launch traced here: 56 us
  Pallas kernels  54.7 us (97%)
  between operations  1.31 us (2%)
    pallas_call x1, Pallas kernels, body(): pl.pallas_call(kernel, out_shape=(out, out), in_specs=[any_space] * 3 + [...  53.8 us

profile of v4, /device:TPU:207, one launch (start us, length us, event | category | flops | bytes accessed | tf_op | source)
XLA Modules:
  0.0 56.0 jit_solution(1833373685066009671)
XLA Ops:
  0.6 0.0 copy-start
  1.3 0.0 copy-done
  1.3 53.8 %frame_attention.1 = (bf16[1,128,1536]{2,1,0:T(8,128)(2,1)S(1)}, bf16[1,128,1536]{2,1,0:T(8,128)(2,1)S(1)}) custom-call(bf16[1,128,1536]{2,1,0:T(8,128)(2,1)} %q_hbm.1, bf16[1,128,1536]{2,1,0:T(8,128)(2,1)} %k_hbm.1, bf16[1,128,1536]{2,1,0:T(8,128)(2,1)} %v_hbm.1, s32[1]{0:T(128)S(6)} %copy.9.levels_hbm, s32[64]{0:T(128)S(1)} %copy-done, ...), custom_call_target="tpu_custom_call" | custom-call | tf_op jit(solution)/shard_map/frame_attention/pallas_call | solution.py:487
  55.1 0.9 %hand_over.1 = (bf16[1,128,1536]{2,1,0:T(8,128)(2,1)}, bf16[1,128,1536]{2,1,0:T(8,128)(2,1)}) custom-call(bf16[1,128,1536]{2,1,0:T(8,128)(2,1)S(1)} %get-tuple-element.4.den_ref, bf16[1,128,1536]{2,1,0:T(8,128)(2,1)S(1)} %get-tuple-element.5.next_ref), custom_call_target="tpu_custom_call" | custom-call | tf_op jit(solution)/shard_map/hand_over/pallas_call | solution.py:511
Async XLA Ops:
  0.6 0.7 %copy-start = (s32[64]{0:T(128)S(1)}, s32[64]{0:T(128)}, u32[]{:S(2)}) copy-start(s32[64]{0:T(128)} %plan_hbm.1) | copy-start | bytes 772

commit v5 on v4

--- a/solution.py
+++ b/solution.py
@@ -413,11 +413,14 @@
     home = [(y_hi + step) % 4 for step in (0, 1, 3, 2)]
     tile_groups = [2 * home[0], 2 * home[0] + 1, 2 * home[1], 2 * home[2] + 1,
                    2 * home[2], 2 * home[1] + 1, 2 * home[3], 2 * home[3] + 1]
-    for k in range(4):
+    for k in range(2):
         finish_tile(k)
-    for pairs in (near_pairs[:1:-1], near_pairs[1::-1]):
+    for n, pairs in enumerate((near_pairs[:1:-1], near_pairs[1::-1])):
         with jax.named_scope("attend_head"):
             attend_heads(pairs)
+        if n == 0:
+            for k in range(2, 4):
+                finish_tile(k)
     with jax.named_scope("sent"):
         @pl.when(has_next)
         def _():

time: 56.2 us -> 56.3 us (level)
  no operation moved by 1% of the time
where the time goes in v5:
time: 56.3 us; the launch traced here: 56.1 us
  Pallas kernels  54.8 us (97%)
  between operations  1.31 us (2%)
    pallas_call x1, Pallas kernels, body(): pl.pallas_call(kernel, out_shape=(out, out), in_specs=[any_space] * 3 + [...  53.9 us

profile of v5, /device:TPU:207, one launch (start us, length us, event | category | flops | bytes accessed | tf_op | source)
XLA Modules:
  0.0 56.1 jit_solution(991702078710788784)
XLA Ops:
  0.6 0.0 copy-start
  1.3 0.0 copy-done
  1.3 53.9 %frame_attention.1 = (bf16[1,128,1536]{2,1,0:T(8,128)(2,1)S(1)}, bf16[1,128,1536]{2,1,0:T(8,128)(2,1)S(1)}) custom-call(bf16[1,128,1536]{2,1,0:T(8,128)(2,1)} %q_hbm.1, bf16[1,128,1536]{2,1,0:T(8,128)(2,1)} %k_hbm.1, bf16[1,128,1536]{2,1,0:T(8,128)(2,1)} %v_hbm.1, s32[1]{0:T(128)S(6)} %copy.9.levels_hbm, s32[64]{0:T(128)S(1)} %copy-done, ...), custom_call_target="tpu_custom_call" | custom-call | tf_op jit(solution)/shard_map/frame_attention/pallas_call | solution.py:490
  55.2 0.9 %hand_over.1 = (bf16[1,128,1536]{2,1,0:T(8,128)(2,1)}, bf16[1,128,1536]{2,1,0:T(8,128)(2,1)}) custom-call(bf16[1,128,1536]{2,1,0:T(8,128)(2,1)S(1)} %get-tuple-element.4.den_ref, bf16[1,128,1536]{2,1,0:T(8,128)(2,1)S(1)} %get-tuple-element.5.next_ref), custom_call_target="tpu_custom_call" | custom-call | tf_op jit(solution)/shard_map/hand_over/pallas_call | solution.py:514
Async XLA Ops:
  0.6 0.7 %copy-start = (s32[64]{0:T(128)S(1)}, s32[64]{0:T(128)}, u32[]{:S(2)}) copy-start(s32[64]{0:T(128)} %plan_hbm.1) | copy-start | bytes 772
